TPU v7x, 256 devices: a whole 4x4x8 slice. The times are simulated.
256 devices in a mesh: row: 8 (over z_lo, y), col: 32 (over z_hi, x, core).
Axes of the slice: x: 4, y: 4, z: 8 (z_hi: 4, z_lo: 2; z = z_hi * 2 + z_lo), core: 2. Of those that a mesh axis runs over, the one named last changes fastest.
Arguments:
- tokens: bfloat16 [512, 12288], P('col', 'row'), may hold values from -6 to 6
- grad_out: bfloat16 [512, 12288], P('col', 'row'), may hold values from -6 to 6
- weight_in: bfloat16 [12288, 24576], P('row', 'col'), may hold values from -0.0546875 to 0.0546875
- weight_out: bfloat16 [24576, 12288], P('col', 'row'), may hold values from -0.0390625 to 0.0390625
Outputs:
- output: bfloat16 [512, 12288], P('col', 'row')
- grad_in: bfloat16 [512, 12288], P('col', 'row')
- grad_w_in: bfloat16 [12288, 24576], P('row', 'col')
- grad_w_out: bfloat16 [24576, 12288], P('col', 'row')
All inputs are finite; a program needn't handle non-finite values.
Results may differ from a plain program's by a relative error of at most 0.02.
Values may be sent and summed in bfloat16 or wider, within the bound.
A program may use at most 64 MiB of HBM per device.

v0:
```python
import math
import jax
import jax.numpy as jnp
from jax import lax
from jax.sharding import PartitionSpec as P

root_two_pi = math.sqrt(2.0 / math.pi)


def gelu_value(pre):
    inner = root_two_pi * (pre + 0.044715 * pre * pre * pre)
    return 0.5 * pre * (1.0 + jnp.tanh(inner))


def gelu_slope(pre):
    inner = root_two_pi * (pre + 0.044715 * pre * pre * pre)
    bent = jnp.tanh(inner)
    return 0.5 * (1.0 + bent) + 0.5 * pre * (1.0 - bent * bent) * root_two_pi * (
        1.0 + 3.0 * 0.044715 * pre * pre
    )


def times_transposed(left, right):
    return lax.dot_general(
        left, right, (((1,), (1,)), ((), ())), preferred_element_type=jnp.float32
    )


def inner_tokens(left, right):
    return lax.dot_general(
        left, right, (((0,), (0,)), ((), ())), preferred_element_type=jnp.float32
    )


def shards(tokens, grad_out, weight_in, weight_out):
    token_panel, grad_panel = (
        lax.all_gather(tokens, "col", axis=0, tiled=True),
        lax.all_gather(grad_out, "col", axis=0, tiled=True),
    )
    total_rows = token_panel.shape[0]
    width_hidden = weight_in.shape[1]
    grad_rows = grad_panel
    forward = jnp.dot(token_panel, weight_in, preferred_element_type=jnp.float32)
    backward = times_transposed(grad_rows, weight_out)
    summed = lax.psum_scatter(
        jnp.concatenate([forward, backward], axis=1), "row", scatter_dimension=0, tiled=True
    )
    hidden_pre = summed[:, :width_hidden]
    hidden_act = gelu_value(hidden_pre).astype(jnp.bfloat16)
    pre_grad = (summed[:, width_hidden:] * gelu_slope(hidden_pre)).astype(jnp.bfloat16)
    act_panel, pregrad_panel = (
        lax.all_gather(hidden_act, "row", axis=0, tiled=True),
        lax.all_gather(pre_grad, "row", axis=0, tiled=True),
    )
    factor = 1.0 / math.sqrt(total_rows)
    output = lax.psum_scatter(
        jnp.dot(act_panel, weight_out, preferred_element_type=jnp.float32).astype(jnp.bfloat16),
        "col",
        scatter_dimension=0,
        tiled=True,
    )
    grad_w_out = (inner_tokens(act_panel, grad_panel) * factor).astype(jnp.bfloat16)
    grad_rows = pregrad_panel
    grad_in = lax.psum_scatter(
        times_transposed(grad_rows, weight_in).astype(jnp.bfloat16),
        "col",
        scatter_dimension=0,
        tiled=True,
    )
    grad_w_in = (inner_tokens(token_panel, pregrad_panel) * factor).astype(jnp.bfloat16)
    return (output, grad_in, grad_w_in, grad_w_out)


def solution(mesh):
    placed = (P("col", "row"), P("col", "row"), P("row", "col"), P("col", "row"))
    return jax.shard_map(
        shards,
        mesh=mesh,
        in_specs=placed,
        out_specs=(P("col", "row"), P("col", "row"), P("row", "col"), P("col", "row")),
        check_vma=False,
    )
```

profile of v0, /device:TPU:8, one launch (start us, length us, event | category | flops | bytes accessed | tf_op | source)
XLA Modules:
  0.0 393.0 jit_solution(12617767968671838270)
XLA Ops:
  7.2 0.0 copy-start
  7.2 0.0 all-gather.5.cloned.1.call-start
  7.2 0.7 all-gather.5.cloned.1.call-update
  7.9 0.0 all-gather.3.cloned.1.call-start
  8.0 0.7 all-gather.3.cloned.1.call-update
  8.7 0.0 reduce-scatter.4.cloned.1.call-start
  8.7 57.9 %all-gather.5.cloned.1.call-done = bf16[512,1536]{1,0:T(8,128)(2,1)} async-done(((bf16[16,1536]{1,0:T(8,128)(2,1)}), bf16[512,1536]{1,0:T(8,128)(2,1)}) %all-gather.5.cloned.1.call-update) | async-done | bytes 1572880 | tf_op jit(solution)/shard_map/all_gather | solution.py:38
  66.6 0.0 copy-done
  66.6 4.0 %fusion.9 = f32[512,768]{1,0:T(8,128)} fusion(bf16[512,1536]{1,0:T(8,128)(2,1)} %all-gather.5.cloned.1.call-done, bf16[768,1536]{1,0:T(8,128)(2,1)S(1)} %copy-done), kind=kOutput, calls=%fused_computation.17 | convolution fusion | flops 1207959552 | bytes 5505024 | tf_op jit(solution)/shard_map/dot_general | solution.py:24
  70.6 48.9 %all-gather.3.cloned.1.call-done = bf16[512,1536]{1,0:T(8,128)(2,1)} async-done(((bf16[16,1536]{1,0:T(8,128)(2,1)}), bf16[512,1536]{1,0:T(8,128)(2,1)}) %all-gather.3.cloned.1.call-update) | async-done | bytes 1572880 | tf_op jit(solution)/shard_map/all_gather | solution.py:37
  119.5 0.0 copy-start.1
  119.5 3.6 fusion.8
  123.1 0.0 copy-done.1
  123.1 2.0 pad_maximum_fusion
  125.1 0.0 reduce-scatter.4.cloned.1.call-update
  125.2 0.0 reduce-scatter.6.cloned.1.call-start
  125.2 44.7 %reduce-scatter.4.cloned.1.call-done = f32[64,1536]{1,0:T(8,128)} async-done(((f32[512,1536]{1,0:T(8,128)}), f32[64,1536]{1,0:T(8,128)}) %reduce-scatter.4.cloned.1.call-update) | async-done | bytes 393232 | tf_op jit(solution)/shard_map/reduce_scatter | solution.py:45
  169.9 1.2 fusion.7
  171.1 29.7 %all_gather.14 = bf16[512,768]{1,0:T(8,128)(2,1)S(1)} all-gather(bf16[64,768]{1,0:T(8,128)(2,1)S(1)} %get-tuple-element.9), channel_id=1, replica_groups=mesh['row'=8,'col'=32] {'row'}, dimensions={0}, use_global_device_ids=true | all-gather | bytes 884736 | tf_op jit(solution)/shard_map/all_gather | solution.py:52
  200.8 2.5 convolution_convert_fusion.1
  203.3 0.0 reduce-scatter.6.cloned.1.call-update
  203.3 0.0 reduce-scatter.8.cloned.1.call-start
  203.4 29.7 %all_gather.15 = bf16[512,768]{1,0:T(8,128)(2,1)S(1)} all-gather(bf16[64,768]{1,0:T(8,128)(2,1)S(1)} %get-tuple-element.8), channel_id=1, replica_groups=mesh['row'=8,'col'=32] {'row'}, dimensions={0}, use_global_device_ids=true | all-gather | bytes 884736 | tf_op jit(solution)/shard_map/all_gather | solution.py:53
  233.1 0.0 copy-start.2
  233.1 0.9 copy-done.2
  233.9 4.3 %convolution_convert_fusion = bf16[512,1536]{1,0:T(8,128)(2,1)} fusion(bf16[512,768]{1,0:T(8,128)(2,1)S(1)} %all_gather.15, bf16[1536,768]{1,0:T(8,128)(2,1)} %param.6), kind=kOutput, calls=%fused_computation.4 | convolution fusion | flops 1208745984 | bytes 4718592 | tf_op jit(solution)/shard_map/dot_general | solution.py:24
  238.2 0.0 reduce-scatter.8.cloned.1.call-update
  238.2 4.5 %fusion = bf16[1536,768]{0,1:T(8,128)(2,1)} fusion(bf16[512,768]{1,0:T(8,128)(2,1)} %copy-done.2, bf16[512,1536]{1,0:T(8,128)(2,1)} %all-gather.3.cloned.1.call-done), kind=kOutput, calls=%fused_computation.3 | convolution fusion | flops 1210318848 | bytes 4718592 | tf_op jit(solution)/shard_map/dot_general | solution.py:30
  242.7 4.3 %copy.8 = bf16[1536,768]{1,0:T(8,128)(2,1)} copy(bf16[1536,768]{0,1:T(8,128)(2,1)} %fusion) | data formatting | bytes 4718592
  247.0 4.2 %multiply_convert_fusion = bf16[768,1536]{1,0:T(8,128)(2,1)} fusion(bf16[512,768]{1,0:T(8,128)(2,1)S(1)} %all_gather.14, bf16[512,1536]{1,0:T(8,128)(2,1)} %all-gather.5.cloned.1.call-done), kind=kOutput, calls=%fused_computation | convolution fusion | flops 1210318848 | bytes 4718592 | tf_op jit(solution)/shard_map/dot_general | solution.py:30
  251.2 43.1 %reduce-scatter.6.cloned.1.call-done = bf16[16,1536]{1,0:T(8,128)(2,1)} async-done(((bf16[512,1536]{1,0:T(8,128)(2,1)}), bf16[16,1536]{1,0:T(8,128)(2,1)}) %reduce-scatter.6.cloned.1.call-update) | async-done | bytes 49168 | tf_op jit(solution)/shard_map/reduce_scatter | solution.py:56
  294.4 92.1 %reduce-scatter.8.cloned.1.call-done = bf16[16,1536]{1,0:T(8,128)(2,1)} async-done(((bf16[512,1536]{1,0:T(8,128)(2,1)}), bf16[16,1536]{1,0:T(8,128)(2,1)}) %reduce-scatter.8.cloned.1.call-update) | async-done | bytes 49168 | tf_op jit(solution)/shard_map/reduce_scatter | solution.py:64
Async XLA Ops:
  7.2 59.4 %copy-start = (bf16[768,1536]{1,0:T(8,128)(2,1)S(1)}, bf16[768,1536]{1,0:T(8,128)(2,1)}, u32[]{:S(2)}) copy-start(bf16[768,1536]{1,0:T(8,128)(2,1)} %param.7) | copy-start | bytes 7077892
  7.2 59.4 %all-gather.5.cloned.1.call-start = ((), (), s32[]{:S(2)}) async-start(), calls=%async_computation.4 | async-start | bytes 1622016 | tf_op jit(solution)/shard_map/all_gather | solution.py:38
  7.9 111.6 %all-gather.3.cloned.1.call-start = ((), (), s32[]{:S(2)}) async-start(), calls=%async_computation.3 | async-start | bytes 1622016 | tf_op jit(solution)/shard_map/all_gather | solution.py:37
  8.7 161.2 %reduce-scatter.4.cloned.1.call-start = ((), (), s32[]{:S(2)}) async-start(), calls=%async_computation.5 | async-start | bytes 3538944 | tf_op jit(solution)/shard_map/reduce_scatter | solution.py:45
  119.5 3.6 copy-start.1
  125.2 169.2 %reduce-scatter.6.cloned.1.call-start = ((), (), s32[]{:S(2)}) async-start(), calls=%async_computation.6 | async-start | bytes 1622016 | tf_op jit(solution)/shard_map/reduce_scatter | solution.py:56
  203.3 183.1 %reduce-scatter.8.cloned.1.call-start = ((), (), s32[]{:S(2)}) async-start(), calls=%async_computation.7 | async-start | bytes 1622016 | tf_op jit(solution)/shard_map/reduce_scatter | solution.py:64
  233.1 0.9 copy-start.2
Sparse Core Ops, SparseCore 0:
  10.6 55.9 all-gather.4
  69.1 50.2 all-gather.2
  125.3 44.5 reduce-scatter.3
  203.5 90.8 reduce-scatter.5
  298.6 87.7 reduce-scatter.7
where the time goes:
time: 393 us
  waiting for transfers between devices  288 us (73%)
  blocking collectives  59.4 us (15%)
  matrix products  23.1 us (6%)
  between operations  13.8 us (4%)
  local copies, waits for them, and re-layouts  5.16 us (1%)
    reduce_scatter x1, waiting for transfers between devices, shards(): lax.psum_scatter(times_transposed(grad_rows, weight_in).astype(jnp.bfloat...  92.1 us
    all_gather x1, waiting for transfers between devices, shards(): lax.all_gather(grad_out, 'col', axis=0, tiled=True)  57.9 us
    all_gather x1, waiting for transfers between devices, shards(): lax.all_gather(tokens, 'col', axis=0, tiled=True)  48.9 us
    reduce_scatter x1, waiting for transfers between devices, shards(): lax.psum_scatter(jnp.concatenate([forward, backward], axis=1), 'row', sca...  44.7 us
    reduce_scatter x1, waiting for transfers between devices, shards(): lax.psum_scatter(jnp.dot(act_panel, weight_out, preferred_element_type=jn...  43.1 us
    all_gather x1, blocking collectives, shards(): lax.all_gather(hidden_act, 'row', axis=0, tiled=True)  29.7 us
    all_gather x1, blocking collectives, shards(): lax.all_gather(pre_grad, 'row', axis=0, tiled=True)  29.7 us
    dot_general x2, matrix products, inner_tokens(): lax.dot_general(left, right, (((0,), (0,)), ((), ())), preferred_element_...  8.73 us
  transfers between devices with their start and end apart: 5, of which 5 were waited for; matrix products, arithmetic and copies ran while one was open for 5% of the time, Pallas kernels for 0%

commit v1 on v0

--- a/solution.py
+++ b/solution.py
@@ -35,7 +35,9 @@
 def shards(tokens, grad_out, weight_in, weight_out):
     token_panel, grad_panel = (
         lax.all_gather(tokens, "col", axis=0, tiled=True),
-        lax.all_gather(grad_out, "col", axis=0, tiled=True),
+        jnp.concatenate(
+            lax.all_to_all(jnp.stack([grad_out] * lax.axis_size("col")), "col", 0, 0), axis=0
+        ),
     )
     total_rows = token_panel.shape[0]
     width_hidden = weight_in.shape[1]

time: 393 us -> 359 us (0.913)
  waiting for transfers between devices: 288 us -> 240 us
  starting transfers between devices: 0.2 us -> 11.6 us
    all_gather x1 -> x0, waiting for transfers between devices: 57.9 us -> none  [shards(): lax.all_gather(grad_out, 'col', axis=0, tiled=True)]
    all_to_all x0 -> x1, waiting for transfers between devices: none -> 38.8 us  [shards(): lax.all_to_all(jnp.stack([grad_out] * lax.axis_size('col')), 'col', 0, 0)]
    all_gather x1, waiting for transfers between devices: 48.9 us -> 20.8 us  [shards(): lax.all_gather(tokens, 'col', axis=0, tiled=True)]
    all_to_all x0 -> x1, starting transfers between devices: none -> 11.4 us  [shards(): lax.all_to_all(jnp.stack([grad_out] * lax.axis_size('col')), 'col', 0, 0)]
  transfers between devices with their start and end apart: 5 -> 5, of which waited for: 5 -> 5; matrix products, arithmetic and copies ran while one was open for 5% -> 6% of each run, Pallas kernels for 0% -> 0%
where the time goes in v1:
time: 359 us
  waiting for transfers between devices  240 us (67%)
  blocking collectives  59.4 us (17%)
  matrix products  23.1 us (6%)
  between operations  13.8 us (4%)
  starting transfers between devices  11.6 us (3%)
  local copies, waits for them, and re-layouts  7.43 us (2%)
    reduce_scatter x1, waiting for transfers between devices, shards(): lax.psum_scatter(times_transposed(grad_rows, weight_in).astype(jnp.bfloat...  92.1 us
    reduce_scatter x1, waiting for transfers between devices, shards(): lax.psum_scatter(jnp.concatenate([forward, backward], axis=1), 'row', sca...  44.7 us
    reduce_scatter x1, waiting for transfers between devices, shards(): lax.psum_scatter(jnp.dot(act_panel, weight_out, preferred_element_type=jn...  43.2 us
    all_to_all x1, waiting for transfers between devices, shards(): lax.all_to_all(jnp.stack([grad_out] * lax.axis_size('col')), 'col', 0, 0)  38.8 us
    all_gather x1, blocking collectives, shards(): lax.all_gather(hidden_act, 'row', axis=0, tiled=True)  29.8 us
    all_gather x1, blocking collectives, shards(): lax.all_gather(pre_grad, 'row', axis=0, tiled=True)  29.7 us
    all_gather x1, waiting for transfers between devices, shards(): lax.all_gather(tokens, 'col', axis=0, tiled=True)  20.8 us
    all_to_all x1, starting transfers between devices, shards(): lax.all_to_all(jnp.stack([grad_out] * lax.axis_size('col')), 'col', 0, 0)  11.4 us
  transfers between devices with their start and end apart: 5, of which 5 were waited for; matrix products, arithmetic and copies ran while one was open for 6% of the time, Pallas kernels for 0%

profile of v1, /device:TPU:8, one launch (start us, length us, event | category | flops | bytes accessed | tf_op | source)
XLA Modules:
  0.0 358.9 jit_solution(12613587689214695184)
XLA Ops:
  7.2 0.0 copy-start
  7.2 2.3 stack.2
  9.4 11.4 %all-to-all-start = ((bf16[32,16,1536]{2,1,0:T(8,128)(2,1)}), bf16[32,16,1536]{2,1,0:T(8,128)(2,1)}, u32[]{:S(2)}, u32[]{:S(2)}) async-start(bf16[32,16,1536]{2,1,0:T(8,128)(2,1)} %stack.2), calls=%async_computation | async-start | bytes 3145728 | tf_op jit(solution)/shard_map/all_to_all | solution.py:39
  20.9 0.0 all-gather.2.cloned.1.call-start
  20.9 0.7 all-gather.2.cloned.1.call-update
  21.6 0.0 reduce-scatter.4.cloned.1.call-start
  21.7 38.8 %all-to-all-done = bf16[32,16,1536]{2,1,0:T(8,128)(2,1)} async-done(((bf16[32,16,1536]{2,1,0:T(8,128)(2,1)}), bf16[32,16,1536]{2,1,0:T(8,128)(2,1)}, u32[]{:S(2)}, u32[]{:S(2)}) %all-to-all-start) | async-done | bytes 1572896 | tf_op jit(solution)/shard_map/all_to_all | solution.py:39
  60.5 0.0 copy-done
  60.5 4.0 %fusion.9 = f32[512,768]{1,0:T(8,128)} fusion(bf16[512,1536]{1,0:T(8,128)(2,1)} %bitcast, bf16[768,1536]{1,0:T(8,128)(2,1)S(1)} %copy-done), kind=kOutput, calls=%fused_computation.17 | convolution fusion | flops 1207959552 | bytes 5505024 | tf_op jit(solution)/shard_map/dot_general | solution.py:24
  64.4 20.8 %all-gather.2.cloned.1.call-done = bf16[512,1536]{1,0:T(8,128)(2,1)} async-done(((bf16[16,1536]{1,0:T(8,128)(2,1)}), bf16[512,1536]{1,0:T(8,128)(2,1)}) %all-gather.2.cloned.1.call-update) | async-done | bytes 1572880 | tf_op jit(solution)/shard_map/all_gather | solution.py:37
  85.2 0.0 copy-start.1
  85.2 3.6 %fusion.8 = f32[512,768]{1,0:T(8,128)S(1)} fusion(bf16[512,1536]{1,0:T(8,128)(2,1)} %all-gather.2.cloned.1.call-done, bf16[1536,768]{1,0:T(8,128)(2,1)} %param.6), kind=kOutput, calls=%fused_computation.16 | convolution fusion | flops 1207959552 | bytes 5505024 | tf_op jit(solution)/shard_map/dot_general | solution.py:45
  88.8 0.0 copy-done.1
  88.9 2.0 pad_maximum_fusion
  90.9 0.0 reduce-scatter.4.cloned.1.call-update
  90.9 0.0 reduce-scatter.6.cloned.1.call-start
  90.9 44.7 %reduce-scatter.4.cloned.1.call-done = f32[64,1536]{1,0:T(8,128)} async-done(((f32[512,1536]{1,0:T(8,128)}), f32[64,1536]{1,0:T(8,128)}) %reduce-scatter.4.cloned.1.call-update) | async-done | bytes 393232 | tf_op jit(solution)/shard_map/reduce_scatter | solution.py:47
  135.7 1.2 fusion.7
  136.8 29.8 %all_gather.10 = bf16[512,768]{1,0:T(8,128)(2,1)S(1)} all-gather(bf16[64,768]{1,0:T(8,128)(2,1)S(1)} %get-tuple-element.9), channel_id=1, replica_groups=mesh['row'=8,'col'=32] {'row'}, dimensions={0}, use_global_device_ids=true | all-gather | bytes 884736 | tf_op jit(solution)/shard_map/all_gather | solution.py:54
  166.6 2.5 convolution_convert_fusion.1
  169.1 0.0 reduce-scatter.6.cloned.1.call-update
  169.2 0.0 reduce-scatter.8.cloned.1.call-start
  169.2 29.7 %all_gather.11 = bf16[512,768]{1,0:T(8,128)(2,1)S(1)} all-gather(bf16[64,768]{1,0:T(8,128)(2,1)S(1)} %get-tuple-element.8), channel_id=1, replica_groups=mesh['row'=8,'col'=32] {'row'}, dimensions={0}, use_global_device_ids=true | all-gather | bytes 884736 | tf_op jit(solution)/shard_map/all_gather | solution.py:55
  198.9 0.0 copy-start.2
  198.9 0.9 copy-done.2
  199.8 4.3 %convolution_convert_fusion = bf16[512,1536]{1,0:T(8,128)(2,1)} fusion(bf16[512,768]{1,0:T(8,128)(2,1)S(1)} %all_gather.11, bf16[1536,768]{1,0:T(8,128)(2,1)} %param.6), kind=kOutput, calls=%fused_computation.4 | convolution fusion | flops 1208745984 | bytes 4718592 | tf_op jit(solution)/shard_map/dot_general | solution.py:24
  204.0 0.0 reduce-scatter.8.cloned.1.call-update
  204.1 4.5 %fusion = bf16[1536,768]{0,1:T(8,128)(2,1)} fusion(bf16[512,768]{1,0:T(8,128)(2,1)} %copy-done.2, bf16[512,1536]{1,0:T(8,128)(2,1)} %all-gather.2.cloned.1.call-done), kind=kOutput, calls=%fused_computation.3 | convolution fusion | flops 1210318848 | bytes 4718592 | tf_op jit(solution)/shard_map/dot_general | solution.py:30
  208.6 4.3 %copy.8 = bf16[1536,768]{1,0:T(8,128)(2,1)} copy(bf16[1536,768]{0,1:T(8,128)(2,1)} %fusion) | data formatting | bytes 4718592
  212.8 4.2 %multiply_convert_fusion = bf16[768,1536]{1,0:T(8,128)(2,1)} fusion(bf16[512,768]{1,0:T(8,128)(2,1)S(1)} %all_gather.10, bf16[512,1536]{1,0:T(8,128)(2,1)} %bitcast), kind=kOutput, calls=%fused_computation | convolution fusion | flops 1210318848 | bytes 4718592 | tf_op jit(solution)/shard_map/dot_general | solution.py:30
  217.1 43.2 %reduce-scatter.6.cloned.1.call-done = bf16[16,1536]{1,0:T(8,128)(2,1)} async-done(((bf16[512,1536]{1,0:T(8,128)(2,1)}), bf16[16,1536]{1,0:T(8,128)(2,1)}) %reduce-scatter.6.cloned.1.call-update) | async-done | bytes 49168 | tf_op jit(solution)/shard_map/reduce_scatter | solution.py:58
  260.3 92.1 %reduce-scatter.8.cloned.1.call-done = bf16[16,1536]{1,0:T(8,128)(2,1)} async-done(((bf16[512,1536]{1,0:T(8,128)(2,1)}), bf16[16,1536]{1,0:T(8,128)(2,1)}) %reduce-scatter.8.cloned.1.call-update) | async-done | bytes 49168 | tf_op jit(solution)/shard_map/reduce_scatter | solution.py:66
Async XLA Ops:
  7.2 53.3 %copy-start = (bf16[768,1536]{1,0:T(8,128)(2,1)S(1)}, bf16[768,1536]{1,0:T(8,128)(2,1)}, u32[]{:S(2)}) copy-start(bf16[768,1536]{1,0:T(8,128)(2,1)} %param.7) | copy-start | bytes 7077892
  9.4 51.0 %all-to-all-start = ((bf16[32,16,1536]{2,1,0:T(8,128)(2,1)}), bf16[32,16,1536]{2,1,0:T(8,128)(2,1)}, u32[]{:S(2)}, u32[]{:S(2)}) async-start(bf16[32,16,1536]{2,1,0:T(8,128)(2,1)} %stack.2), calls=%async_computation | async-start | bytes 3145728 | tf_op jit(solution)/shard_map/all_to_all | solution.py:39
  20.9 64.3 %all-gather.2.cloned.1.call-start = ((), (), s32[]{:S(2)}) async-start(), calls=%async_computation.4 | async-start | bytes 1622016 | tf_op jit(solution)/shard_map/all_gather | solution.py:37
  21.6 114.0 %reduce-scatter.4.cloned.1.call-start = ((), (), s32[]{:S(2)}) async-start(), calls=%async_computation.5 | async-start | bytes 3538944 | tf_op jit(solution)/shard_map/reduce_scatter | solution.py:47
  85.2 3.6 %copy-start.1 = (f32[512,768]{1,0:T(8,128)S(1)}, f32[512,768]{1,0:T(8,128)}, u32[]{:S(2)}) copy-start(f32[512,768]{1,0:T(8,128)} %fusion.9) | copy-start | bytes 4718596
  90.9 169.4 %reduce-scatter.6.cloned.1.call-start = ((), (), s32[]{:S(2)}) async-start(), calls=%async_computation.6 | async-start | bytes 1622016 | tf_op jit(solution)/shard_map/reduce_scatter | solution.py:58
  169.2 183.3 %reduce-scatter.8.cloned.1.call-start = ((), (), s32[]{:S(2)}) async-start(), calls=%async_computation.7 | async-start | bytes 1622016 | tf_op jit(solution)/shard_map/reduce_scatter | solution.py:66
  198.9 0.9 copy-start.2
Sparse Core Ops, SparseCore 0:
  24.3 60.8 all-gather.1
  91.0 44.6 reduce-scatter.3
  169.3 90.9 reduce-scatter.5
  264.6 87.8 reduce-scatter.7
